TPU v7x, 32 devices: a whole 2x2x4 slice. The times are simulated.
32 devices in a mesh: probe: 4 (over z), sx: 4 (over x, core), sy: 2 (over y).
Axes of the slice: x: 2, y: 2, z: 4, core: 2. Of those that a mesh axis runs over, the one named last changes fastest.
Arguments:
- probes: float32 [8, 128, 64, 256], P('probe', 'sx', 'sy'), may hold values from -6 to 6
- velocity: float32 [3, 128, 64, 256], P(None, 'sx', 'sy'), may hold values from -0.15 to 0.15
- diffusivity: float32 [128, 64, 256], P('sx', 'sy'), may hold values from 0.02 to 0.15
- obs_weight: float32 [128, 64, 256], P('sx', 'sy'), may hold values from 0.05 to 1
Outputs:
- basis_fields: float32 [8, 128, 64, 256], P('probe', 'sx', 'sy')
- projected_hessian: float32 [8, 8], replicated
All inputs are finite; a program needn't handle non-finite values.
Results may differ from a plain program's by a relative error of at most 0.00013.
Values sent between devices are 32-bit elements; how exact they have to be, the bound alone decides.
No kernel may reach another device: no remote copies, remote signals or barrier semaphores. Data moves between devices by JAX's collectives and lax.ppermute only.
A program may use at most 128 MiB of HBM per device.

v0:
```python
import jax
import jax.numpy as jnp
from jax import lax
from jax.sharding import PartitionSpec as P

STEPS = 4


def extended(value, sides, width):
    for axis, dim in sides:
        devices, length = (lax.axis_size(axis), value.shape[dim])
        up = [(i, (i + 1) % devices) for i in range(devices - 1)]
        down = [(j, i) for i, j in up]
        last = lax.slice_in_dim(value, length - width, length, axis=dim)
        leading = lax.slice_in_dim(value, 0, width, axis=dim)
        before = lax.ppermute(last, axis, up)
        after = lax.ppermute(leading, axis, down)
        value = jnp.concatenate([before, value, after], axis=dim)
    return value


def forward_step(state, coeffs):
    cc = coeffs[:, 1:-1, 1:-1, :]
    spread = cc[0]
    inner = state[:, 1:-1, 1:-1, :]
    padded = jnp.pad(inner, ((0, 0), (0, 0), (0, 0), (1, 1)))
    result = (1.0 - 6.0 * spread) * inner
    result = (
        result
        + (spread - 0.5 * cc[1]) * state[:, 2:, 1:-1, :]
        + (spread + 0.5 * cc[1]) * state[:, :-2, 1:-1, :]
    )
    result = (
        result
        + (spread - 0.5 * cc[2]) * state[:, 1:-1, 2:, :]
        + (spread + 0.5 * cc[2]) * state[:, 1:-1, :-2, :]
    )
    result = (
        result
        + (spread - 0.5 * cc[3]) * padded[..., 2:]
        + (spread + 0.5 * cc[3]) * padded[..., :-2]
    )
    return result


def adjoint_step(state, coeffs):
    spread = coeffs[0]
    plus_x = (spread - 0.5 * coeffs[1]) * state
    minus_x = (spread + 0.5 * coeffs[1]) * state
    plus_y = (spread - 0.5 * coeffs[2]) * state
    minus_y = (spread + 0.5 * coeffs[2]) * state
    cc = coeffs[:, 1:-1, 1:-1, :]
    inner = state[:, 1:-1, 1:-1, :]
    pad_plus = jnp.pad((cc[0] - 0.5 * cc[3]) * inner, ((0, 0), (0, 0), (0, 0), (1, 1)))
    pad_minus = jnp.pad((cc[0] + 0.5 * cc[3]) * inner, ((0, 0), (0, 0), (0, 0), (1, 1)))
    result = (1.0 - 6.0 * cc[0]) * inner
    result = result + plus_x[:, :-2, 1:-1, :] + minus_x[:, 2:, 1:-1, :]
    result = result + plus_y[:, 1:-1, :-2, :] + minus_y[:, 1:-1, 2:, :]
    result = result + pad_plus[..., :-2] + pad_minus[..., 2:]
    return result


def crop_one(coeffs):
    return coeffs[:, 1:-1, 1:-1, :]


def factor_inverse(gram, count):
    lower = jnp.linalg.cholesky(gram)
    return jax.scipy.linalg.solve_triangular(lower, jnp.eye(count, dtype=jnp.float32), lower=True)


def shards(probes, velocity, diffusivity, obs_weight):
    group = probes.shape[0]
    count = group * lax.axis_size("probe")
    ncells = (
        probes.shape[1]
        * probes.shape[2]
        * probes.shape[3]
        * lax.axis_size("sx")
        * lax.axis_size("sy")
    )
    coeffs = jnp.concatenate([diffusivity[None], velocity], axis=0)
    highest = lax.Precision.HIGHEST
    wide_coeffs = extended(coeffs, (("sx", 1), ("sy", 2)), STEPS)

    def hessian(field):
        state = extended(field, (("sx", 1), ("sy", 2)), STEPS)
        current = wide_coeffs
        for step in range(STEPS):
            state = forward_step(state, current)
            current = crop_one(current)
        state = obs_weight * state
        state = extended(state, (("sx", 1), ("sy", 2)), STEPS)
        current = wide_coeffs
        for step in range(STEPS):
            state = adjoint_step(state, current)
            current = crop_one(current)
        return state

    images = hessian(probes)
    slabs = lax.all_to_all(images, "probe", split_axis=1, concat_axis=0, tiled=True)
    flat = slabs.reshape(count, -1)
    partial_gram = jnp.dot(flat, flat.T, precision=highest)
    gram = lax.psum(partial_gram, ("probe", "sx", "sy")) / ncells
    inverse = factor_inverse(gram, count)
    basis_slab = jnp.dot(inverse, flat, precision=highest)
    basis_fields = lax.all_to_all(
        basis_slab.reshape(slabs.shape), "probe", split_axis=0, concat_axis=1, tiled=True
    )
    second = hessian(basis_fields)
    second_slab = lax.all_to_all(second, "probe", split_axis=1, concat_axis=0, tiled=True).reshape(
        count, -1
    )
    partial_ritz = jnp.dot(basis_slab, second_slab.T, precision=highest)
    projected = lax.psum(partial_ritz, ("probe", "sx", "sy")) / ncells
    return (basis_fields, projected)


def solution(mesh):
    return jax.shard_map(
        shards,
        mesh=mesh,
        in_specs=(
            P("probe", "sx", "sy", None),
            P(None, "sx", "sy", None),
            P("sx", "sy", None),
            P("sx", "sy", None),
        ),
        out_specs=(P("probe", "sx", "sy", None), P()),
        check_vma=False,
    )
```

profile of v0, /device:TPU:0, one launch (start us, length us, event | category | flops | bytes accessed | tf_op | source)
XLA Modules:
  0.0 581.6 jit_solution(16331773079816440260)
XLA Ops:
  2.1 2.5 collective-permute-start
  7.4 5.1 collective-permute-start.4
  19.2 4.6 collective-permute-start.2
  37.3 7.5 %collective-permute-done.6 = f32[2,40,4,256]{3,1,2,0:T(8,128)S(1)} collective-permute-done((f32[2,40,4,256]{3,1,2,0:T(8,128)S(1)}, f32[2,40,4,256]{3,1,2,0:T(8,128)S(1)}, u32[]{:S(2)}, u32[]{:S(2)}) %collective-permute-start.6) | collective-permute-done | bytes 327712 | tf_op jit(solution)/shard_map/ppermute | solution.py:16
  45.3 2.0 slice.787
  49.4 4.0 subtract_bitcast_fusion.13
  53.4 3.9 subtract_bitcast_fusion.9
  58.3 3.0 copy.47
  81.1 1.7 copy.49
  87.6 2.0 copy.55
  92.9 9.4 %fusion.6 = f32[2,38,38,256]{3,1,2,0:T(8,128)S(1)} fusion(f32[2,38,38,256]{3,1,2,0:T(8,128)} %slice.787, f32[2,40,40,256]{3,1,2,0:T(8,128)S(1)} %pad_maximum_fusion.1, f32[38,38,256]{2,0,1:T(8,128)} %copy.59, f32[38,38,256]{2,0,1:T(8,128)} %copy.58, f32[38,38,256]{2,0,1:T(8,128)} %copy.57, f32[38,38,256]{2,0,1:T(8,128)} %copy.56, f32[38,38,256]{2,0,1:T(8,128)} %copy.55, ...), kind=kLoop, calls=%fused_computation.43 | loop fusion | flops 9611264 | bytes 28094464 | tf_op jit(solution)/shard_map/add | solution.py:39
  102.4 1.9 slice.795
  104.3 8.4 %fusion.34 = f32[2,36,36,256]{3,1,2,0:T(8,128)S(1)} fusion(f32[2,36,36,256]{3,1,2,0:T(8,128)} %slice.795, f32[2,38,38,256]{3,1,2,0:T(8,128)S(1)} %fusion.6, f32[36,36,256]{2,0,1:T(8,128)S(1)} %copy-done.7, f32[36,36,256]{2,0,1:T(8,128)} %copy.64, f32[36,36,256]{2,0,1:T(8,128)} %copy.63, f32[36,36,256]{2,0,1:T(8,128)} %copy.62, f32[36,36,256]{2,0,1:T(8,128)} %copy.61, ...), kind=kLoop, calls=%fused_computation.87 | loop fusion | flops 8626176 | bytes 25214976 | tf_op jit(solution)/shard_map/add | solution.py:39
  112.7 1.8 slice.803
  115.4 7.6 %fusion.62 = f32[2,34,34,256]{3,1,2,0:T(8,128)S(1)} fusion(f32[2,34,34,256]{3,1,2,0:T(8,128)} %slice.803, f32[2,36,36,256]{3,1,2,0:T(8,128)S(1)} %fusion.34, f32[34,34,256]{2,0,1:T(8,128)S(1)} %copy-done.19, f32[34,34,256]{2,0,1:T(8,128)} %copy.70, f32[34,34,256]{2,0,1:T(8,128)} %copy.69, f32[34,34,256]{2,0,1:T(8,128)} %copy.68, f32[34,34,256]{2,0,1:T(8,128)} %copy.67, ...), kind=kLoop, calls=%fused_computation.131 | loop fusion | flops 7694336 | bytes 22491136 | tf_op jit(solution)/shard_map/add | solution.py:39
  125.2 4.5 fusion.91
  129.9 3.3 collective-permute-start.8
  149.1 4.1 collective-permute-start.10
  160.5 1.7 copy.100
  162.2 2.2 collective-permute-done.11
  165.0 3.6 slice_multiply_fusion.50
  169.2 5.9 %fusion.1 = f32[2,38,38,256]{3,1,2,0:T(8,128)S(1)} fusion(f32[2,38,38,256]{3,1,2,0:T(8,128)} %get-tuple-element.48, f32[2,38,38,256]{3,1,2,0:T(8,128)} %get-tuple-element.47, f32[2,40,40,256]{3,1,2,0:T(8,128)S(1)} %pad_maximum_fusion.2, f32[38,38,256]{2,0,1:T(8,128)S(1)} %copy-done.55, f32[38,38,256]{2,0,1:T(8,128)} %copy.100, f32[38,38,256]{2,0,1:T(8,128)} %copy.101, ...), kind=kLoop, calls=%fused_computation.38 | loop fusion | flops 8132608 | bytes 31051776 | tf_op jit(solution)/shard_map/add | solution.py:59
  175.2 3.4 slice_multiply_fusion.54
  179.2 5.4 fusion.29
  184.7 3.4 slice_multiply_fusion.58
  189.3 4.9 fusion.57
  196.8 2.4 fusion.85
  200.4 54.4 %all_to_all.48 = f32[2,32,32,256]{3,2,0,1:T(8,128)S(1)} all-to-all(f32[2,32,32,256]{3,2,0,1:T(8,128)S(1)} %copy.82), channel_id=1, replica_groups=mesh['probe'=4,'sx'=4,'sy'=2] {'probe'}, dimensions={1} | all-to-all | bytes 4194304 | tf_op jit(solution)/shard_map/all_to_all | solution.py:101
  256.2 3.3 reshape.29
  259.5 6.8 %fusion.122 = f32[8,8]{0,1:T(8,128)S(1)} fusion(f32[8,65536]{1,0:T(8,128)} %reshape.29), kind=kOutput, calls=%fused_computation.314 | convolution fusion | flops 50331648 | bytes 2097408 | tf_op jit(solution)/shard_map/dot_general | solution.py:103
  266.3 38.8 %psum.14 = f32[8,8]{0,1:T(8,128)S(1)} all-reduce(f32[8,8]{0,1:T(8,128)S(1)} %fusion.122), channel_id=1, replica_groups=mesh['probe'=4,'sx'=4,'sy'=2] {'probe','sx','sy'}, use_global_device_ids=true, to_apply=%region_0.1 | all-reduce | flops 64 | bytes 512 | tf_op jit(solution)/shard_map/psum | solution.py:104
  308.1 3.4 fusion.123
  312.2 50.4 %all_to_all.49 = f32[8,8,32,256]{3,2,1,0:T(8,128)S(1)} all-to-all(f32[8,8,32,256]{3,2,1,0:T(8,128)S(1)} %copy.87), channel_id=1, replica_groups=mesh['probe'=4,'sx'=4,'sy'=2] {'probe'}, dimensions={0} | all-to-all | bytes 4194304 | tf_op jit(solution)/shard_map/all_to_all | solution.py:107
  366.5 3.7 collective-permute-done.13
  370.4 3.4 collective-permute-start.14
  373.8 1.7 collective-permute-start.15
  375.5 2.9 collective-permute-done.14
  378.3 4.4 collective-permute-done.15
  383.2 2.0 slice.859
  386.2 7.7 %fusion.10 = f32[2,38,38,256]{3,1,2,0:T(8,128)S(1)} fusion(f32[2,38,38,256]{3,1,2,0:T(8,128)} %slice.859, f32[2,40,40,256]{3,1,2,0:T(8,128)S(1)} %pad_maximum_fusion.3, f32[38,38,256]{2,0,1:T(8,128)S(1)} %copy-done.2, f32[38,38,256]{2,0,1:T(8,128)S(1)} %copy-done.4, f32[38,38,256]{2,0,1:T(8,128)S(1)} %copy-done.39, f32[38,38,256]{2,0,1:T(8,128)} %copy.56, ...), kind=kLoop, calls=%fused_computation.47 | loop fusion | flops 9611264 | bytes 28094464 | tf_op jit(solution)/shard_map/add | solution.py:39
  393.9 1.9 slice.864
  396.8 7.9 %fusion.38 = f32[2,36,36,256]{3,1,2,0:T(8,128)S(1)} fusion(f32[2,36,36,256]{3,1,2,0:T(8,128)} %slice.864, f32[2,38,38,256]{3,1,2,0:T(8,128)S(1)} %fusion.10, f32[36,36,256]{2,0,1:T(8,128)S(1)} %copy-done.9, f32[36,36,256]{2,0,1:T(8,128)S(1)} %copy-done.11, f32[36,36,256]{2,0,1:T(8,128)} %copy.63, f32[36,36,256]{2,0,1:T(8,128)} %copy.62, ...), kind=kLoop, calls=%fused_computation.91 | loop fusion | flops 8626176 | bytes 25214976 | tf_op jit(solution)/shard_map/add | solution.py:39
  404.7 1.8 slice.869
  407.5 7.6 %fusion.66 = f32[2,34,34,256]{3,1,2,0:T(8,128)S(1)} fusion(f32[2,34,34,256]{3,1,2,0:T(8,128)} %slice.869, f32[2,36,36,256]{3,1,2,0:T(8,128)S(1)} %fusion.38, f32[34,34,256]{2,0,1:T(8,128)S(1)} %copy-done.21, f32[34,34,256]{2,0,1:T(8,128)} %copy.70, f32[34,34,256]{2,0,1:T(8,128)} %copy.69, f32[34,34,256]{2,0,1:T(8,128)} %copy.68, f32[34,34,256]{2,0,1:T(8,128)} %copy.67, ...), kind=kLoop, calls=%fused_computation.135 | loop fusion | flops 7694336 | bytes 22491136 | tf_op jit(solution)/shard_map/add | solution.py:39
  417.3 4.3 fusion.96
  421.6 5.3 collective-permute-start.16
  428.2 2.9 collective-permute-done.17
  434.1 3.1 collective-permute-done.18
  437.2 4.4 collective-permute-done.19
  442.1 3.2 slice_multiply_fusion.48
  445.3 6.1 %fusion.3 = f32[2,38,38,256]{3,1,2,0:T(8,128)S(1)} fusion(f32[2,38,38,256]{3,1,2,0:T(8,128)} %get-tuple-element.46, f32[2,38,38,256]{3,1,2,0:T(8,128)} %get-tuple-element.45, f32[2,40,40,256]{3,1,2,0:T(8,128)S(1)} %pad_maximum_fusion.4, f32[38,38,256]{2,0,1:T(8,128)} %copy.99, f32[38,38,256]{2,0,1:T(8,128)} %copy.100, f32[38,38,256]{2,0,1:T(8,128)} %copy.101, ...), kind=kLoop, calls=%fused_computation.40 | loop fusion | flops 8132608 | bytes 31051776 | tf_op jit(solution)/shard_map/add | solution.py:59
  451.5 3.6 slice_multiply_fusion.52
  456.7 5.0 fusion.31
  461.8 2.0 slice_multiply_fusion.56
  465.8 4.4 fusion.59
  472.6 2.4 fusion.87
  475.1 2.5 copy.89
  477.6 4.8 all-to-all-start.2
  482.4 2.5 copy.92
  485.0 46.1 %all-to-all-done.2 = f32[2,32,32,256]{3,2,0,1:T(8,128)} async-done(((f32[2,32,32,256]{3,2,0,1:T(8,128)}), f32[2,32,32,256]{3,2,0,1:T(8,128)}, u32[]{:S(2)}, u32[]{:S(2)}) %all-to-all-start.2) | async-done | bytes 2097184 | tf_op jit(solution)/shard_map/all_to_all | solution.py:111
  531.0 3.2 copy.103
  534.2 3.4 reshape.31
  537.6 6.2 %fusion.124 = f32[8,8]{0,1:T(8,128)S(1)} fusion(f32[8,65536]{1,0:T(8,128)S(1)} %copy-done.52, f32[8,65536]{1,0:T(8,128)} %reshape.31), kind=kOutput, calls=%fused_computation.316 | convolution fusion | flops 50331648 | bytes 4194560 | tf_op jit(solution)/shard_map/dot_general | solution.py:114
  543.8 36.9 %psum.15 = f32[8,8]{0,1:T(8,128)S(1)} all-reduce(f32[8,8]{0,1:T(8,128)S(1)} %fusion.124), channel_id=1, replica_groups=mesh['probe'=4,'sx'=4,'sy'=2] {'probe','sx','sy'}, use_global_device_ids=true, to_apply=%region_3.4 | all-reduce | flops 64 | bytes 512 | tf_op jit(solution)/shard_map/psum | solution.py:115
  (298 shorter events, 114.8 us)
Async XLA Ops:
  0.6 5.4 copy-start.91
  2.1 12.0 %copy-start.25 = (f32[32,32,256]{2,1,0:T(8,128)S(1)}, f32[32,32,256]{2,1,0:T(8,128)}, u32[]{:S(2)}) copy-start(f32[32,32,256]{2,1,0:T(8,128)} %param.6) | copy-start | bytes 3145732
  2.1 15.3 %collective-permute-start = (f32[4,4,32,256]{3,2,1,0:T(8,128)S(1)}, f32[4,4,32,256]{3,2,1,0:T(8,128)S(1)}, u32[]{:S(2)}, u32[]{:S(2)}) collective-permute-start(f32[4,4,32,256]{3,2,1,0:T(8,128)S(1)} %get-tuple-element.43), channel_id=1, source_target_pairs={{0,2},{2,4},{4,6},{1,3},{3,5},{5,7},{8,10},{10,12},{12,14},{9,11},... | collective-permute-start | bytes 1572872 | tf_op jit(solution)/shard_map/ppermute | solution.py:16
  4.6 9.6 %copy-start.92 = (f32[32,32,256]{2,1,0:T(8,128)S(1)}, f32[32,32,256]{2,1,0:T(8,128)}, u32[]{:S(2)}) copy-start(f32[32,32,256]{2,1,0:T(8,128)} %param.7) | copy-start | bytes 3145732
  4.6 12.8 %collective-permute-start.1 = (f32[4,4,32,256]{3,2,1,0:T(8,128)S(1)}, f32[4,4,32,256]{3,2,1,0:T(8,128)S(1)}, u32[]{:S(2)}, u32[]{:S(2)}) collective-permute-start(f32[4,4,32,256]{3,2,1,0:T(8,128)S(1)} %get-tuple-element.44), channel_id=1, source_target_pairs={{2,0},{4,2},{6,4},{3,1},{5,3},{7,5},{10,8},{12,10},{14,12},{11,9},... | collective-permute-start | bytes 1572872 | tf_op jit(solution)/shard_map/ppermute | solution.py:17
  7.4 16.5 %collective-permute-start.4 = (f32[2,4,32,256]{3,1,2,0:T(4,128)S(1)}, f32[2,4,32,256]{3,1,2,0:T(4,128)S(1)}, u32[]{:S(2)}, u32[]{:S(2)}) collective-permute-start(f32[2,4,32,256]{3,1,2,0:T(4,128)S(1)} %get-tuple-element.75), channel_id=1, source_target_pairs={{0,2},{2,4},{4,6},{1,3},{3,5},{5,7},{8,10},{10,12},{12,14},{9,11},... | collective-permute-start | bytes 786440 | tf_op jit(solution)/shard_map/ppermute | solution.py:16
  12.5 4.9 copy-start
  12.5 11.3 %collective-permute-start.5 = (f32[2,4,32,256]{3,1,2,0:T(4,128)S(1)}, f32[2,4,32,256]{3,1,2,0:T(4,128)S(1)}, u32[]{:S(2)}, u32[]{:S(2)}) collective-permute-start(f32[2,4,32,256]{3,1,2,0:T(4,128)S(1)} %get-tuple-element.76), channel_id=1, source_target_pairs={{2,0},{4,2},{6,4},{3,1},{5,3},{7,5},{10,8},{12,10},{14,12},{11,9},... | collective-permute-start | bytes 786440 | tf_op jit(solution)/shard_map/ppermute | solution.py:17
  17.9 29.4 %collective-permute-start.3 = (f32[4,40,4,256]{3,1,2,0:T(8,128)S(1)}, f32[4,40,4,256]{3,1,2,0:T(8,128)S(1)}, u32[]{:S(2)}, u32[]{:S(2)}) collective-permute-start(f32[4,40,4,256]{3,1,2,0:T(8,128)S(1)} %copy.44), channel_id=1, source_target_pairs={{1,0},{3,2},{5,4},{7,6},{9,8},{11,10},{13,12},{15,14},{17,16},{19,... | collective-permute-start | bytes 1966088 | tf_op jit(solution)/shard_map/ppermute | solution.py:17
  19.2 28.4 %collective-permute-start.2 = (f32[4,40,4,256]{3,1,2,0:T(8,128)S(1)}, f32[4,40,4,256]{3,1,2,0:T(8,128)S(1)}, u32[]{:S(2)}, u32[]{:S(2)}) collective-permute-start(f32[4,40,4,256]{3,1,2,0:T(8,128)S(1)} %copy.43), channel_id=1, source_target_pairs={{0,1},{2,3},{4,5},{6,7},{8,9},{10,11},{12,13},{14,15},{16,17},{18,... | collective-permute-start | bytes 1966088 | tf_op jit(solution)/shard_map/ppermute | solution.py:16
  24.0 20.9 %collective-permute-start.6 = (f32[2,40,4,256]{3,1,2,0:T(8,128)S(1)}, f32[2,40,4,256]{3,1,2,0:T(8,128)S(1)}, u32[]{:S(2)}, u32[]{:S(2)}) collective-permute-start(f32[2,40,4,256]{3,1,2,0:T(8,128)S(1)} %get-tuple-element.67), channel_id=1, source_target_pairs={{0,1},{2,3},{4,5},{6,7},{8,9},{10,11},{12,13},{14,15},{16,17},{18,... | collective-permute-start | bytes 983048 | tf_op jit(solution)/shard_map/ppermute | solution.py:16
  25.3 19.5 %collective-permute-start.7 = (f32[2,40,4,256]{3,1,2,0:T(8,128)S(1)}, f32[2,40,4,256]{3,1,2,0:T(8,128)S(1)}, u32[]{:S(2)}, u32[]{:S(2)}) collective-permute-start(f32[2,40,4,256]{3,1,2,0:T(8,128)S(1)} %get-tuple-element.68), channel_id=1, source_target_pairs={{1,0},{3,2},{5,4},{7,6},{9,8},{11,10},{13,12},{15,14},{17,16},{19,... | collective-permute-start | bytes 983048 | tf_op jit(solution)/shard_map/ppermute | solution.py:17
  58.3 4.5 copy-start.89
  70.2 3.2 copy-start.82
  125.2 9.4 %copy-start.47 = (f32[34,34,256]{2,0,1:T(8,128)S(1)}, f32[34,34,256]{2,0,1:T(8,128)}, u32[]{:S(2)}) copy-start(f32[34,34,256]{2,0,1:T(8,128)} %copy.69) | copy-start | bytes 3551236
  129.8 6.0 %copy-start.48 = (f32[34,34,256]{2,0,1:T(8,128)S(1)}, f32[34,34,256]{2,0,1:T(8,128)}, u32[]{:S(2)}) copy-start(f32[34,34,256]{2,0,1:T(8,128)} %copy.67) | copy-start | bytes 3551236
  129.8 7.1 %copy-start.49 = (f32[34,34,256]{2,0,1:T(8,128)S(1)}, f32[34,34,256]{2,0,1:T(8,128)}, u32[]{:S(2)}) copy-start(f32[34,34,256]{2,0,1:T(8,128)} %copy.68) | copy-start | bytes 3551236
  129.9 19.1 %collective-permute-start.8 = (f32[2,4,32,256]{3,1,2,0:T(4,128)S(1)}, f32[2,4,32,256]{3,1,2,0:T(4,128)S(1)}, u32[]{:S(2)}, u32[]{:S(2)}) collective-permute-start(f32[2,4,32,256]{3,1,2,0:T(4,128)S(1)} %get-tuple-element.73), channel_id=1, source_target_pairs={{0,2},{2,4},{4,6},{1,3},{3,5},{5,7},{8,10},{10,12},{12,14},{9,11},... | collective-permute-start | bytes 786440 | tf_op jit(solution)/shard_map/ppermute | solution.py:16
  133.2 4.8 copy-start.50
  133.2 15.8 %collective-permute-start.9 = (f32[2,4,32,256]{3,1,2,0:T(4,128)S(1)}, f32[2,4,32,256]{3,1,2,0:T(4,128)S(1)}, u32[]{:S(2)}, u32[]{:S(2)}) collective-permute-start(f32[2,4,32,256]{3,1,2,0:T(4,128)S(1)} %get-tuple-element.74), channel_id=1, source_target_pairs={{2,0},{4,2},{6,4},{3,1},{5,3},{7,5},{10,8},{12,10},{14,12},{11,9},... | collective-permute-start | bytes 786440 | tf_op jit(solution)/shard_map/ppermute | solution.py:17
  135.7 3.4 copy-start.43
  149.1 13.2 %collective-permute-start.10 = (f32[2,40,4,256]{3,1,2,0:T(8,128)S(1)}, f32[2,40,4,256]{3,1,2,0:T(8,128)S(1)}, u32[]{:S(2)}, u32[]{:S(2)}) collective-permute-start(f32[2,40,4,256]{3,1,2,0:T(8,128)S(1)} %get-tuple-element.65), channel_id=1, source_target_pairs={{0,1},{2,3},{4,5},{6,7},{8,9},{10,11},{12,13},{14,15},{16,17},{18,... | collective-permute-start | bytes 983048 | tf_op jit(solution)/shard_map/ppermute | solution.py:16
  153.2 11.3 %collective-permute-start.11 = (f32[2,40,4,256]{3,1,2,0:T(8,128)S(1)}, f32[2,40,4,256]{3,1,2,0:T(8,128)S(1)}, u32[]{:S(2)}, u32[]{:S(2)}) collective-permute-start(f32[2,40,4,256]{3,1,2,0:T(8,128)S(1)} %get-tuple-element.66), channel_id=1, source_target_pairs={{1,0},{3,2},{5,4},{7,6},{9,8},{11,10},{13,12},{15,14},{17,16},{19,... | collective-permute-start | bytes 983048 | tf_op jit(solution)/shard_map/ppermute | solution.py:17
  164.9 3.6 copy-start.1
  165.0 3.6 copy-start.53
  165.0 4.3 copy-start.55
  169.2 5.9 %copy-start.8 = (f32[36,36,256]{2,0,1:T(8,128)S(1)}, f32[36,36,256]{2,0,1:T(8,128)}, u32[]{:S(2)}) copy-start(f32[36,36,256]{2,0,1:T(8,128)} %copy.65) | copy-start | bytes 3981316
  169.2 5.9 %copy-start.10 = (f32[36,36,256]{2,0,1:T(8,128)S(1)}, f32[36,36,256]{2,0,1:T(8,128)}, u32[]{:S(2)}) copy-start(f32[36,36,256]{2,0,1:T(8,128)} %copy.64) | copy-start | bytes 3981316
  175.1 3.4 copy-start.13
  175.1 3.4 copy-start.56
  175.2 4.0 copy-start.58
  179.2 5.4 copy-start.20
  179.2 5.4 copy-start.23
  184.7 3.4 copy-start.16
  184.7 3.4 copy-start.62
  184.7 3.8 copy-start.64
  184.7 4.6 copy-start.66
  189.3 5.0 copy-start.27
  189.3 5.0 copy-start.31
  311.5 51.1 %copy-start.51 = (f32[8,65536]{1,0:T(8,128)}, f32[8,65536]{1,0:T(8,128)S(1)}, u32[]{:S(2)}) copy-start(f32[8,65536]{1,0:T(8,128)S(1)} %fusion.123) | copy-start | bytes 6291460
  363.8 19.4 %copy-start.5 = (f32[4,2,8,32,256]{4,2,0,3,1:T(8,128)}, f32[4,2,8,32,256]{4,2,0,3,1:T(8,128)S(1)}, u32[]{:S(2)}) copy-start(f32[4,2,8,32,256]{4,2,0,3,1:T(8,128)S(1)} %copy.104) | copy-start | bytes 6291460
  363.9 2.6 collective-permute-start.12
  365.2 5.0 collective-permute-start.13
  370.4 7.9 %collective-permute-start.14 = (f32[2,40,4,256]{3,1,2,0:T(8,128)S(1)}, f32[2,40,4,256]{3,1,2,0:T(8,128)S(1)}, u32[]{:S(2)}, u32[]{:S(2)}) collective-permute-start(f32[2,40,4,256]{3,1,2,0:T(8,128)S(1)} %get-tuple-element.63), channel_id=1, source_target_pairs={{0,1},{2,3},{4,5},{6,7},{8,9},{10,11},{12,13},{14,15},{16,17},{18,... | collective-permute-start | bytes 983048 | tf_op jit(solution)/shard_map/ppermute | solution.py:16
  373.8 9.0 %collective-permute-start.15 = (f32[2,40,4,256]{3,1,2,0:T(8,128)S(1)}, f32[2,40,4,256]{3,1,2,0:T(8,128)S(1)}, u32[]{:S(2)}, u32[]{:S(2)}) collective-permute-start(f32[2,40,4,256]{3,1,2,0:T(8,128)S(1)} %get-tuple-element.64), channel_id=1, source_target_pairs={{1,0},{3,2},{5,4},{7,6},{9,8},{11,10},{13,12},{15,14},{17,16},{19,... | collective-permute-start | bytes 983048 | tf_op jit(solution)/shard_map/ppermute | solution.py:17
  421.6 6.6 %collective-permute-start.16 = (f32[2,4,32,256]{3,1,2,0:T(4,128)S(1)}, f32[2,4,32,256]{3,1,2,0:T(4,128)S(1)}, u32[]{:S(2)}, u32[]{:S(2)}) collective-permute-start(f32[2,4,32,256]{3,1,2,0:T(4,128)S(1)} %get-tuple-element.69), channel_id=1, source_target_pairs={{0,2},{2,4},{4,6},{1,3},{3,5},{5,7},{8,10},{10,12},{12,14},{9,11},... | collective-permute-start | bytes 786440 | tf_op jit(solution)/shard_map/ppermute | solution.py:16
  426.9 4.2 collective-permute-start.17
  431.2 6.0 %collective-permute-start.18 = (f32[2,40,4,256]{3,1,2,0:T(8,128)S(1)}, f32[2,40,4,256]{3,1,2,0:T(8,128)S(1)}, u32[]{:S(2)}, u32[]{:S(2)}) collective-permute-start(f32[2,40,4,256]{3,1,2,0:T(8,128)S(1)} %get-tuple-element.61), channel_id=1, source_target_pairs={{0,1},{2,3},{4,5},{6,7},{8,9},{10,11},{12,13},{14,15},{16,17},{18,... | collective-permute-start | bytes 983048 | tf_op jit(solution)/shard_map/ppermute | solution.py:16
  432.7 9.0 %collective-permute-start.19 = (f32[2,40,4,256]{3,1,2,0:T(8,128)S(1)}, f32[2,40,4,256]{3,1,2,0:T(8,128)S(1)}, u32[]{:S(2)}, u32[]{:S(2)}) collective-permute-start(f32[2,40,4,256]{3,1,2,0:T(8,128)S(1)} %get-tuple-element.62), channel_id=1, source_target_pairs={{1,0},{3,2},{5,4},{7,6},{9,8},{11,10},{13,12},{15,14},{17,16},{19,... | collective-permute-start | bytes 983048 | tf_op jit(solution)/shard_map/ppermute | solution.py:17
  445.3 6.1 %copy-start.12 = (f32[36,36,256]{2,0,1:T(8,128)S(1)}, f32[36,36,256]{2,0,1:T(8,128)}, u32[]{:S(2)}) copy-start(f32[36,36,256]{2,0,1:T(8,128)} %copy.64) | copy-start | bytes 3981316
  451.4 3.6 copy-start.14
  451.4 3.6 copy-start.57
  451.4 4.0 copy-start.59
  451.4 4.8 copy-start.60
  451.4 5.2 copy-start.61
  456.7 5.0 copy-start.22
  456.7 5.0 copy-start.24
  461.8 3.6 copy-start.67
  461.8 4.0 copy-start.68
  465.8 4.4 copy-start.29
  465.8 4.4 copy-start.33
  477.6 4.8 copy-start.6
  477.6 53.4 %all-to-all-start.2 = ((f32[2,32,32,256]{3,2,0,1:T(8,128)}), f32[2,32,32,256]{3,2,0,1:T(8,128)}, u32[]{:S(2)}, u32[]{:S(2)}) async-start(f32[2,32,32,256]{3,2,0,1:T(8,128)} %copy.89), calls=%async_computation.2 | async-start | bytes 4194304 | tf_op jit(solution)/shard_map/all_to_all | solution.py:111
  534.2 3.4 copy-start.52
  (50 other events, 116.4 us)
where the time goes:
time: 591 us; the launch traced here: 582 us
  blocking collectives  180 us (30%)
  other arithmetic  133 us (23%)
  local copies, waits for them, and re-layouts  121 us (20%)
  waiting for transfers between devices  77.2 us (13%)
  starting transfers between devices  51.4 us (9%)
  matrix products  16.6 us (3%)
    all_to_all x1, blocking collectives, shards(): lax.all_to_all(images, 'probe', split_axis=1, concat_axis=0, tiled=True)  54.4 us
    all_to_all x1, blocking collectives, shards(): lax.all_to_all(basis_slab.reshape(slabs.shape), 'probe', split_axis=0, co...  50.4 us
    add x6, other arithmetic, forward_step(): result + (spread - 0.5 * cc[3]) * padded[..., 2:]  48.6 us
    all_to_all x1, waiting for transfers between devices, shards(): lax.all_to_all(second, 'probe', split_axis=1, concat_axis=0, tiled=True)  46.1 us
    psum x1, blocking collectives, shards(): gram = lax.psum(partial_gram, ('probe', 'sx', 'sy')) / ncells  38.8 us
    psum x1, blocking collectives, shards(): projected = lax.psum(partial_ritz, ('probe', 'sx', 'sy')) / ncells  36.9 us
    add x8, other arithmetic, adjoint_step(): result = result + pad_plus[..., :-2] + pad_minus[..., 2:]  36.5 us
    ppermute x10, starting transfers between devices, extended(): before = lax.ppermute(last, axis, up)  32.4 us
  transfers between devices with their start and end apart: 21, of which 9 were waited for; matrix products, arithmetic and copies ran while one was open for 7% of the time, Pallas kernels for 0%

commit v1 on v0

v1 whole, which is shorter than its diff:
```python
import functools

import jax
import jax.numpy as jnp
from jax import lax
from jax.experimental import pallas as pl
from jax.experimental.pallas import tpu as pltpu
from jax.sharding import PartitionSpec as P

STEPS = 4
SUB = 8
LANES = 128
VMEM_LIMIT = 58 * 1024 * 1024


def vmem_call(body, outs, scratch, ins, flops, smem_first=True):
    specs = [pl.BlockSpec(memory_space=pltpu.VMEM)] * len(ins)
    if smem_first:
        specs[0] = pl.BlockSpec(memory_space=pltpu.SMEM)
    size = sum(4 * a.size for a in list(ins) + list(outs))
    return pl.pallas_call(
        body,
        out_shape=outs,
        in_specs=specs,
        out_specs=[pl.BlockSpec(memory_space=pltpu.VMEM)] * len(outs),
        scratch_shapes=scratch,
        compiler_params=pltpu.CompilerParams(vmem_limit_bytes=VMEM_LIMIT),
        cost_estimate=pl.CostEstimate(flops=flops, bytes_accessed=size, transcendentals=0),
    )(*ins)


def f32(*shape):
    return jax.ShapeDtypeStruct(shape, jnp.float32)


def strip_shapes(fields, x, y, z, both):
    packs = [f32(fields, x // 2, SUB, z), f32(fields, 2, SUB, z), f32(fields, 2, SUB, z)]
    return [f32(fields, STEPS, y, z)] * 2 + packs * (2 if both else 1)


def write_strips(tile, field, outs, side):
    x, y, z = outs[2].shape[1] * 2, outs[0].shape[2], outs[0].shape[3]
    for i in range(STEPS):
        outs[0][field, i] = tile(i, slice(0, y))
        outs[1][field, i] = tile(x - STEPS + i, slice(0, y))
    row = lax.broadcasted_iota(jnp.int32, (SUB, z), 0)
    both = len(outs) > 5

    def packed(i):
        first_lo, second_lo = tile(2 * i, slice(0, SUB)), tile(2 * i + 1, slice(0, SUB))
        first_hi, second_hi = tile(2 * i, slice(y - SUB, y)), tile(2 * i + 1, slice(y - SUB, y))
        lo = jnp.where(row < STEPS, first_lo, pltpu.roll(second_lo, STEPS, 0))
        hi = jnp.where(row < STEPS, pltpu.roll(first_hi, STEPS, 0), second_hi)
        return [lo, hi] if both else [jnp.where(side == 0, hi, lo)]

    def step(i, carry):
        for n, value in enumerate(packed(i)):
            outs[2 + 3 * n][field, i] = value
        return carry

    lax.fori_loop(0, x // 2, step, None)
    for n in range(2 if both else 1):
        for i in range(2):
            outs[3 + 3 * n][field, i] = outs[2 + 3 * n][field, i]
            outs[4 + 3 * n][field, i] = outs[2 + 3 * n][field, x // 2 - 2 + i]


def exchange(strips):
    nx, ny = lax.axis_size("sx"), lax.axis_size("sy")
    up = [(i, i + 1) for i in range(nx - 1)]
    down = [(j, i) for i, j in up]

    def moved(value, dx, dys):
        pairs = []
        for i in range(nx):
            for j in range(ny):
                for dy in dys(j):
                    if 0 <= i + dx < nx and 0 <= j + dy < ny:
                        pairs.append((i * ny + j, (i + dx) * ny + j + dy))
        return lax.ppermute(value, ("sx", "sy"), pairs)

    below = lax.ppermute(strips[1], "sx", up)
    above = lax.ppermute(strips[0], "sx", down)
    received = [below, above]
    if len(strips) == 5:
        flip = lambda j: (1 - 2 * j,)
        pack, corner_lo, corner_hi = strips[2:]
        received += [moved(pack, 0, flip), moved(corner_hi, 1, flip), moved(corner_lo, -1, flip)]
    else:
        for n, dy in ((0, -1), (1, 1)):
            pack, corner_lo, corner_hi = strips[2 + 3 * n : 5 + 3 * n]
            one = lambda j, dy=dy: (dy,)
            received += [moved(pack, 0, one), moved(corner_hi, 1, one), moved(corner_lo, -1, one)]
    return received


def assemble(dst, tile, field, received, side):
    x, y, z = received[2].shape[1] * 2, received[0].shape[2], received[0].shape[3]

    def copy(i, carry):
        dst(i, slice(0, y), tile(i))
        return carry

    lax.fori_loop(0, x, copy, None)
    for i in range(STEPS):
        dst(x + i, slice(0, y), received[1][field, i])
        dst(x + STEPS + i, slice(0, y), received[0][field, i])
    row = lax.broadcasted_iota(jnp.int32, (SUB, z), 0)
    both = len(received) > 5

    def put(at, packs):
        if both:
            hi, lo = packs
        else:
            hi = jnp.where(side == 0, packs[0], 0.0)
            lo = jnp.where(side == 0, 0.0, packs[0])
        dst(at, slice(y, y + SUB), jnp.where(row < STEPS, hi, pltpu.roll(lo, STEPS, 0)))
        dst(at + 1, slice(y, y + SUB), jnp.where(row < STEPS, pltpu.roll(hi, STEPS, 0), lo))

    groups = [received[2:5]] + ([received[5:8]] if both else [])

    def main(i, carry):
        put(2 * i, [g[0][field, i] for g in groups])
        return carry

    lax.fori_loop(0, x // 2, main, None)
    for i in range(2):
        put(x + 2 * i, [g[2][field, i] for g in groups])
        put(x + STEPS + 2 * i, [g[1][field, i] for g in groups])


def coefficient_rows(coef):
    _, wide, rows, z = coef.shape
    lane = lax.broadcasted_iota(jnp.int32, (rows, z), 1)

    def row(i, carry):
        spread = coef[0, i]
        for d in range(3):
            half = 0.5 * coef[1 + 2 * d, i]
            plus, minus = spread - half, spread + half
            if d == 2:
                plus = jnp.where(lane == z - 1, 0.0, plus)
                minus = jnp.where(lane == 0, 0.0, minus)
            coef[1 + 2 * d, i] = plus
            coef[2 + 2 * d, i] = minus
        coef[0, i] = 1.0 - 6.0 * spread
        return carry

    lax.fori_loop(0, wide, row, None)


def sweep(coef, src, step, adjoint, tile_rows, write):
    fields, wide, rows, z = src.shape
    x = wide - 2 * STEPS
    reach = STEPS - 1 - step
    chunks, cols = rows // SUB, z // LANES
    done = tile_rows // SUB if step == STEPS - 1 else chunks
    sub = lax.broadcasted_iota(jnp.int32, (SUB, LANES), 0)
    lane = lax.broadcasted_iota(jnp.int32, (SUB, LANES), 1)
    first_row, last_row = sub == 0, sub == SUB - 1
    first_lane, last_lane = lane == 0, lane == LANES - 1

    def piece(ref, lead, xi, c, j):
        return ref[lead, xi, SUB * c : SUB * (c + 1), LANES * j : LANES * (j + 1)]

    def body(i, carry):
        wrap = lambda a: jnp.where(a < 0, a + wide, a)
        here, back, ahead = wrap(i), wrap(i - 1), wrap(i + 1)
        value, up, down = {}, {}, {}

        def state(p, c, j):
            if (p, c, j) not in value:
                value[p, c, j] = piece(src, p, here, c, j)
            return value[p, c, j]

        def shifted(p, c, j):
            key = (p, c % chunks, j)
            if key not in up:
                u = state(*key)
                if adjoint:
                    up[key] = pltpu.roll(piece(coef, 4, here, key[1], j) * u, SUB - 1, 0)
                    down[key] = pltpu.roll(piece(coef, 3, here, key[1], j) * u, 1, 0)
                else:
                    up[key] = pltpu.roll(u, SUB - 1, 0)
                    down[key] = pltpu.roll(u, 1, 0)
            return up[key], down[key]

        for c in range(done):
            for p in range(fields):
                us = [state(p, c, j) for j in range(cols)]
                if adjoint:
                    plus = [pltpu.roll(piece(coef, 6, here, c, j) * us[j], LANES - 1, 1) for j in range(cols)]
                    minus = [pltpu.roll(piece(coef, 5, here, c, j) * us[j], 1, 1) for j in range(cols)]
                else:
                    plus = [pltpu.roll(us[j], LANES - 1, 1) for j in range(cols)]
                    minus = [pltpu.roll(us[j], 1, 1) for j in range(cols)]
                for j in range(cols):
                    yp = jnp.where(last_row, shifted(p, c + 1, j)[0], shifted(p, c, j)[0])
                    ym = jnp.where(first_row, shifted(p, c - 1, j)[1], shifted(p, c, j)[1])
                    zp = jnp.where(last_lane, plus[(j + 1) % cols], plus[j])
                    zm = jnp.where(first_lane, minus[j - 1], minus[j])
                    xp, xm = piece(src, p, ahead, c, j), piece(src, p, back, c, j)
                    if adjoint:
                        xs = piece(coef, 2, ahead, c, j) * xp + piece(coef, 1, back, c, j) * xm
                        ys, zs = yp + ym, zp + zm
                    else:
                        xs = piece(coef, 1, here, c, j) * xp + piece(coef, 2, here, c, j) * xm
                        ys = piece(coef, 3, here, c, j) * yp + piece(coef, 4, here, c, j) * ym
                        zs = piece(coef, 5, here, c, j) * zp + piece(coef, 6, here, c, j) * zm
                    write(p, here, c, j, (piece(coef, 0, here, c, j) * us[j] + xs) + (ys + zs))
        return carry

    lax.fori_loop(-reach, x + reach, body, None)


def run_steps(coef, state, out, adjoint, weight=None):
    tile_rows = out.shape[2]
    for step in range(STEPS):
        src, dst = state.at[step % 2], state.at[(step + 1) % 2]

        def write(p, i, c, j, value, dst=dst, last=step == STEPS - 1):
            at = (pl.ds(SUB * c, SUB), pl.ds(LANES * j, LANES))
            if last:
                out[p, i, *at] = value if weight is None else weight[i, *at] * value
            else:
                dst[p, i, *at] = value

        sweep(coef, src, step, adjoint, tile_rows, write)


def pack_kernel(scalars, probes, velocity, diffusivity, *outs):
    side = scalars[0]
    write_strips(lambda i, r: diffusivity[i, r], 0, outs, side)
    for d in range(3):
        write_strips(lambda i, r: velocity[d, i, r], 1 + d, outs, side)
    for p in range(probes.shape[0]):
        write_strips(lambda i, r: probes[p, i, r], 4 + p, outs, side)


def first_kernel(count, scalars, probes, velocity, diffusivity, weight, *refs):
    side = scalars[0]
    received, (coef, out), strips, state = refs[:count], refs[count : count + 2], refs[count + 2 : -1], refs[-1]

    def slot(s):
        def store(i, rows, value):
            coef[s, i, rows] = value
        return store

    assemble(slot(0), lambda i: diffusivity[i], 0, received, side)
    for d in range(3):
        assemble(slot(1 + 2 * d), lambda i: velocity[d, i], 1 + d, received, side)
    coefficient_rows(coef)
    fill_state(state, probes, 4, received, side)
    run_steps(coef, state, out, False, weight)
    for p in range(out.shape[0]):
        write_strips(lambda i, r: out[p, i, r], p, strips, side)


def fill_state(state, tile, offset, received, side):
    for p in range(tile.shape[0]):
        def store(i, rows, value):
            state[0, p, i, rows] = value

        assemble(store, lambda i: tile[p, i], offset + p, received, side)


def next_kernel(count, adjoint, scalars, coef, tile, weight, *refs):
    side = scalars[0]
    received, out, strips, state = refs[:count], refs[count], refs[count + 1 : -1], refs[-1]
    fill_state(state, tile, 0, received, side)
    run_steps(coef, state, out, adjoint, None if adjoint else weight)
    if strips:
        for p in range(out.shape[0]):
            write_strips(lambda i, r: out[p, i, r], p, strips, side)


def dots_kernel(own_group, scalars, images, second, others, out):
    group, x, y, z = images.shape
    chunks, cols = y // SUB, z // LANES
    pairs = [(a, b) for a in range(group) for b in range(group) if not own_group or b <= a]

    def body(i, sums):
        sums = list(sums)
        for c in range(chunks):
            for j in range(cols):
                at = (pl.ds(SUB * c, SUB), pl.ds(LANES * j, LANES))
                other = [others[b, i, *at] for b in range(group)]
                mine = [images[a, i, *at] for a in range(group)]
                then = [second[a, i, *at] for a in range(group)]
                for n, (a, b) in enumerate(pairs):
                    sums[2 * n] = sums[2 * n] + mine[a] * other[b]
                    sums[2 * n + 1] = sums[2 * n + 1] + then[a] * other[b]
        return tuple(sums)

    zero = jnp.zeros((SUB, LANES), jnp.float32)
    sums = lax.fori_loop(0, x, body, (zero,) * (2 * len(pairs)))
    row0, col0 = scalars[1] * group, scalars[2] * group
    count = out.shape[0]
    row = lax.broadcasted_iota(jnp.int32, out.shape, 0)
    lane = lax.broadcasted_iota(jnp.int32, out.shape, 1)
    total = jnp.zeros(out.shape, jnp.float32)
    for n, (a, b) in enumerate(pairs):
        for k in range(2):
            value = jnp.sum(jnp.sum(sums[2 * n + k], axis=0, keepdims=True), axis=1, keepdims=True)
            here = (row == row0 + a) & (lane == col0 + b + k * count) & (scalars[2] >= 0)
            total = total + jnp.where(here, value, 0.0)
    out[...] = total


def basis_kernel(inverse, *refs):
    images, out = refs[:-1], refs[-1]
    group, x, y, z = out.shape
    chunks, cols = y // SUB, z // LANES

    def body(i, carry):
        for c in range(chunks):
            for j in range(cols):
                at = (pl.ds(SUB * c, SUB), pl.ds(LANES * j, LANES))
                sums = [None] * group
                for s, image in enumerate(images):
                    for b in range(group):
                        value = image[b, i, *at]
                        for a in range(group):
                            term = inverse[a, s * group + b] * value
                            sums[a] = term if sums[a] is None else sums[a] + term
                for a in range(group):
                    out[a, i, *at] = sums[a]
        return carry

    lax.fori_loop(0, x, body, None)


def all_sum(value):
    for axis in ("sx", "sy", "probe"):
        devices = lax.axis_size(axis)
        if devices & (devices - 1):
            value = lax.psum(value, axis)
            continue
        bit = 1
        while bit < devices:
            value = value + lax.ppermute(value, axis, [(i, i ^ bit) for i in range(devices)])
            bit *= 2
    return value


def shards(probes, velocity, diffusivity, obs_weight):
    group, x, y, z = probes.shape
    groups = lax.axis_size("probe")
    count = group * groups
    ncells = x * y * z * lax.axis_size("sx") * lax.axis_size("sy")
    both = lax.axis_size("sy") != 2
    side, mine = lax.axis_index("sy"), lax.axis_index("probe")
    cells = group * x * y * z

    def scalars(other):
        return jnp.stack([side, mine, mine - other]).astype(jnp.int32)

    where = scalars(0)
    wide = (x + 2 * STEPS, y + 2 * STEPS, z)
    state = [pltpu.VMEM((2, group) + wide, jnp.float32)]
    tile = f32(group, x, y, z)
    strips2 = strip_shapes(group, x, y, z, both)

    strips = vmem_call(pack_kernel, strip_shapes(4 + group, x, y, z, both), [], [where, probes, velocity, diffusivity], cells)
    received = exchange(strips)
    coef, halfway, *strips = vmem_call(
        functools.partial(first_kernel, len(received)),
        [f32(7, *wide), tile] + strips2,
        state,
        [where, probes, velocity, diffusivity, obs_weight] + received,
        100 * cells,
    )

    def model(field, strips, adjoint, last=False):
        received = exchange(strips)
        return vmem_call(
            functools.partial(next_kernel, len(received), adjoint),
            [tile] + ([] if last else strips2),
            state,
            [where, coef, field, obs_weight] + received,
            70 * cells,
        )

    images, *strips = model(halfway, strips, True)

    right = [(i, i + 1) for i in range(groups - 1)]
    passed = [images]
    for _ in range(groups - 1):
        passed.append(lax.ppermute(passed[-1], "probe", right))

    halfway, *strips = model(images, strips, False)
    (second,) = model(halfway, strips, True, True)

    partial = None
    for n, others in enumerate(passed):
        (part,) = vmem_call(
            functools.partial(dots_kernel, n == 0),
            [f32(count, LANES)],
            [],
            [scalars(n), images, second, others],
            4 * cells,
        )
        partial = part if partial is None else partial + part
    total = all_sum(partial) / ncells
    strict = jnp.tril(jnp.ones((count, count), jnp.float32), -1)
    gram, ritz = total[:, :count], total[:, count : 2 * count]
    gram = gram + (gram * strict).T
    ritz = ritz + (ritz * strict).T
    lower = jnp.linalg.cholesky(gram)
    inverse = jax.scipy.linalg.solve_triangular(lower, jnp.eye(count, dtype=jnp.float32), lower=True)
    highest = lax.Precision.HIGHEST
    projected = jnp.dot(jnp.dot(inverse, ritz, precision=highest), inverse.T, precision=highest)

    rows = lax.dynamic_slice_in_dim(inverse, mine * group, group, 0)
    parts = []
    for n in range(groups):
        part = lax.dynamic_slice_in_dim(rows, jnp.maximum(mine - n, 0) * group, group, 1)
        parts.append(jnp.where(mine >= n, part, 0.0))
    (basis,) = vmem_call(basis_kernel, [tile], [], [jnp.concatenate(parts, 1)] + passed, 2 * count * cells)
    return (basis, projected)


def solution(mesh):
    return jax.shard_map(
        shards,
        mesh=mesh,
        in_specs=(
            P("probe", "sx", "sy", None),
            P(None, "sx", "sy", None),
            P("sx", "sy", None),
            P("sx", "sy", None),
        ),
        out_specs=(P("probe", "sx", "sy", None), P()),
        check_vma=False,
    )
```

time: 591 us -> 385 us (0.65); the launches traced: 582 us -> 384 us
  blocking collectives: 180 us -> 0 us
  Pallas kernels: 0 us -> 166 us
  other arithmetic: 133 us -> 6.72 us
  local copies, waits for them, and re-layouts: 121 us -> 7.4 us
  waiting for transfers between devices: 77.2 us -> 140 us
  matrix products: 16.6 us -> 1.13 us
  starting transfers between devices: 51.4 us -> 62.6 us
    pallas_call x0 -> x10, Pallas kernels: none -> 166 us  [vmem_call(): pl.pallas_call(body, out_shape=outs, in_specs=specs, out_specs=[pl.BlockS...]
    ppermute x20 -> x28, waiting for transfers between devices: 31.1 us -> 140 us  [the longest x3 88.9 us: shards(): passed.append(lax.ppermute(passed[-1], 'probe', right))]
    all_to_all x2 -> x0, blocking collectives: 105 us -> none  [the longest x1 54.4 us: shards(): lax.all_to_all(images, 'probe', split_axis=1, concat_axis=0, tiled=True)]
    add x14 -> x9, other arithmetic: 85.1 us -> 0.82 us  [the longest x2 0.7 us: shards(): partial = part if partial is None else partial + part]
    psum x2 -> x0, blocking collectives: 75.7 us -> none  [the longest x1 38.8 us: shards(): gram = lax.psum(partial_gram, ('probe', 'sx', 'sy')) / ncells]
    all_to_all x1 -> x0, waiting for transfers between devices: 46.1 us -> none  [shards(): lax.all_to_all(second, 'probe', split_axis=1, concat_axis=0, tiled=True)]
    mul x27 -> x0, local copies, waits for them, and re-layouts: 44.2 us -> none  [the longest x4 6.71 us: forward_step(): (spread + 0.5 * cc[1]) * state[:, :-2, 1:-1, :]]
    mul x15 -> x0, other arithmetic: 39.7 us -> none  [the longest x8 20.3 us: adjoint_step(): (cc[0] + 0.5 * cc[3]) * inner]
  transfers between devices with their start and end apart: 21 -> 28, of which waited for: 9 -> 15; matrix products, arithmetic and copies ran while one was open for 7% -> 1% of each run, Pallas kernels for 0% -> 21%
where the time goes in v1:
time: 385 us; the launch traced here: 384 us
  Pallas kernels  166 us (43%)
  waiting for transfers between devices  140 us (36%)
  starting transfers between devices  62.6 us (16%)
  local copies, waits for them, and re-layouts  7.4 us (2%)
  other arithmetic  6.72 us (2%)
    pallas_call x10, Pallas kernels, vmem_call(): pl.pallas_call(body, out_shape=outs, in_specs=specs, out_specs=[pl.BlockS...  166 us
    ppermute x3, waiting for transfers between devices, shards(): passed.append(lax.ppermute(passed[-1], 'probe', right))  88.9 us
    ppermute x12, waiting for transfers between devices, moved(): return lax.ppermute(value, ('sx', 'sy'), pairs)  36.6 us
    ppermute x12, starting transfers between devices, moved(): return lax.ppermute(value, ('sx', 'sy'), pairs)  26.6 us
    ppermute x3, starting transfers between devices, shards(): passed.append(lax.ppermute(passed[-1], 'probe', right))  15 us
    ppermute x5, waiting for transfers between devices, all_sum(): lax.ppermute(value, axis, [(i, i ^ bit) for i in range(devices)])  14.4 us
    ppermute x4, starting transfers between devices, exchange(): below = lax.ppermute(strips[1], 'sx', up)  9.02 us
  transfers between devices with their start and end apart: 28, of which 15 were waited for; matrix products, arithmetic and copies ran while one was open for 1% of the time, Pallas kernels for 21%

profile of v1, /device:TPU:0, one launch (start us, length us, event | category | flops | bytes accessed | tf_op | source)
XLA Modules:
  0.0 384.3 jit_solution(13886697769239003436)
XLA Ops:
  1.2 5.0 %shard_map.59 = (f32[6,4,32,256]{3,2,1,0:T(8,128)}, f32[6,4,32,256]{3,2,1,0:T(8,128)}, f32[6,16,8,256]{3,2,1,0:T(8,128)}, f32[6,2,8,256]{3,2,1,0:T(8,128)}, f32[6,2,8,256]{3,2,1,0:T(8,128)}) custom-call(s32[3]{0:T(128)} %pad_add_fusion.scalars, f32[2,32,32,256]{3,2,1,0:T(8,128)} %probes.3, f32[3,32,32,256]{3,2,1,0:T(8,128)} %velocity.3, ...), custom_call_target="tpu_custom_call" | custom-call | flops 524288 | bytes 8847372 | tf_op jit(solution)/shard_map/pallas_call | solution.py:21
  6.2 2.4 collective-permute-start
  8.6 1.3 collective-permute-start.1
  9.9 2.4 collective-permute-start.2
  12.4 4.1 %collective-permute-start.3 = (f32[6,2,8,256]{3,2,1,0:T(8,128)}, f32[6,2,8,256]{3,2,1,0:T(8,128)S(1)}, u32[]{:S(2)}, u32[]{:S(2)}) collective-permute-start(f32[6,2,8,256]{3,2,1,0:T(8,128)} %get-tuple-element.29), channel_id=1, source_target_pairs={{0,3},{1,2},{2,5},{3,4},{4,7},{5,6},{8,11},{9,10},{10,13},{11,12},... | collective-permute-start | bytes 294920 | tf_op jit(solution)/shard_map/ppermute | solution.py:80
  16.5 1.3 collective-permute-start.4
  17.8 14.6 %collective-permute-done.3.refs_3_ = f32[6,2,8,256]{3,2,1,0:T(8,128)S(1)} collective-permute-done((f32[6,2,8,256]{3,2,1,0:T(8,128)}, f32[6,2,8,256]{3,2,1,0:T(8,128)S(1)}, u32[]{:S(2)}, u32[]{:S(2)}) %collective-permute-start.3) | collective-permute-done | bytes 98336 | tf_op jit(solution)/shard_map/ppermute | solution.py:80
  32.3 1.8 collective-permute-done.4.refs_4_
  35.4 0.9 copy-done.3
  36.3 37.7 %shard_map.60 = (f32[7,40,40,256]{3,2,1,0:T(8,128)}, f32[2,32,32,256]{3,2,1,0:T(8,128)}, f32[2,4,32,256]{3,2,1,0:T(8,128)}, f32[2,4,32,256]{3,2,1,0:T(8,128)}, f...) custom-call(s32[3]{0:T(128)} %pad_add_fusion.scalars, f32[2,32,32,256]{3,2,1,0:T(8,128)} %probes.3, ...), custom_call_target="tpu_custom_call" | custom-call | flops 52428800 | bytes 24313868 | tf_op jit(solution)/shard_map/pallas_call | solution.py:21
  74.0 1.7 collective-permute-start.5
  75.6 1.3 collective-permute-start.6
  76.9 1.7 collective-permute-start.7
  78.6 4.1 %collective-permute-start.8 = (f32[2,2,8,256]{3,2,1,0:T(8,128)}, f32[2,2,8,256]{3,2,1,0:T(8,128)S(1)}, u32[]{:S(2)}, u32[]{:S(2)}) collective-permute-start(f32[2,2,8,256]{3,2,1,0:T(8,128)} %get-tuple-element.36), channel_id=1, source_target_pairs={{0,3},{1,2},{2,5},{3,4},{4,7},{5,6},{8,11},{9,10},{10,13},{11,12},... | collective-permute-start | bytes 98312 | tf_op jit(solution)/shard_map/ppermute | solution.py:80
  82.7 1.3 collective-permute-start.9
  84.0 2.0 collective-permute-done.8.refs_3_
  86.0 2.4 collective-permute-done.9.refs_4_
  89.3 33.6 %shard_map.61 = (f32[2,32,32,256]{3,2,1,0:T(8,128)}, f32[2,4,32,256]{3,2,1,0:T(8,128)}, f32[2,4,32,256]{3,2,1,0:T(8,128)}, f32[2,16,8,256]{3,2,1,0:T(8,128)}, f3...) custom-call(s32[3]{0:T(128)} %pad_add_fusion.scalars, f32[7,40,40,256]{3,2,1,0:T(8,128)} %get-tuple-element.31.coef, ...), custom_call_target="tpu_custom_call" | custom-call | flops 36700160 | bytes 18415628 | tf_op jit(solution)/shard_map/pallas_call | solution.py:21
  122.9 3.6 collective-permute-start.20
  126.5 44.6 %collective-permute-done.20.others.refs_1_ = f32[2,32,32,256]{3,2,1,0:T(8,128)S(1)} collective-permute-done((f32[2,32,32,256]{3,2,1,0:T(8,128)}, f32[2,32,32,256]{3,2,1,0:T(8,128)S(1)}, u32[]{:S(2)}, u32[]{:S(2)}) %collective-permute-start.20) | collective-permute-done | bytes 2097184 | tf_op jit(solution)/shard_map/ppermute | solution.py:389
  171.1 5.6 %collective-permute-start.21 = (f32[2,32,32,256]{3,2,1,0:T(8,128)S(1)}, f32[2,32,32,256]{3,2,1,0:T(8,128)}, u32[]{:S(2)}, u32[]{:S(2)}) collective-permute-start(f32[2,32,32,256]{3,2,1,0:T(8,128)S(1)} %collective-permute-done.20.others.refs_1_), channel_id=1, source_target_pairs={{0,8},{8,16},{16,24},{1,9},{9,17},{17,25},{2,10},{10,18},{18,26},{... | collective-permute-start | bytes 6291464 | tf_op jit(solution)/shard_map/ppermute | solution.py:389
  176.7 44.3 %collective-permute-done.21.others.refs_2_ = f32[2,32,32,256]{3,2,1,0:T(8,128)} collective-permute-done((f32[2,32,32,256]{3,2,1,0:T(8,128)S(1)}, f32[2,32,32,256]{3,2,1,0:T(8,128)}, u32[]{:S(2)}, u32[]{:S(2)}) %collective-permute-start.21) | collective-permute-done | bytes 2097184 | tf_op jit(solution)/shard_map/ppermute | solution.py:389
  221.0 5.8 %collective-permute-start.22 = (f32[2,32,32,256]{3,2,1,0:T(8,128)}, f32[2,32,32,256]{3,2,1,0:T(8,128)}, u32[]{:S(2)}, u32[]{:S(2)}) collective-permute-start(f32[2,32,32,256]{3,2,1,0:T(8,128)} %collective-permute-done.21.others.refs_2_), channel_id=1, source_target_pairs={{0,8},{8,16},{16,24},{1,9},{9,17},{17,25},{2,10},{10,18},{18,26},{... | collective-permute-start | bytes 6291464 | tf_op jit(solution)/shard_map/ppermute | solution.py:389
  226.8 1.8 collective-permute-start.10
  228.6 1.3 collective-permute-start.11
  229.9 1.9 collective-permute-start.12
  231.8 2.8 collective-permute-start.13
  234.6 4.6 %collective-permute-done.13.refs_3_ = f32[2,2,8,256]{3,2,1,0:T(8,128)S(1)} collective-permute-done((f32[2,2,8,256]{3,2,1,0:T(8,128)}, f32[2,2,8,256]{3,2,1,0:T(8,128)S(1)}, u32[]{:S(2)}, u32[]{:S(2)}) %collective-permute-start.13) | collective-permute-done | bytes 32800 | tf_op jit(solution)/shard_map/ppermute | solution.py:80
  239.2 1.3 collective-permute-start.14
  240.5 4.2 %collective-permute-done.14.refs_4_ = f32[2,2,8,256]{3,2,1,0:T(8,128)S(1)} collective-permute-done((f32[2,2,8,256]{3,2,1,0:T(8,128)}, f32[2,2,8,256]{3,2,1,0:T(8,128)S(1)}, u32[]{:S(2)}, u32[]{:S(2)}) %collective-permute-start.14) | collective-permute-done | bytes 32800 | tf_op jit(solution)/shard_map/ppermute | solution.py:80
  245.5 0.7 copy-done.11
  246.2 33.2 %shard_map.62 = (f32[2,32,32,256]{3,2,1,0:T(8,128)}, f32[2,4,32,256]{3,2,1,0:T(8,128)}, f32[2,4,32,256]{3,2,1,0:T(8,128)}, f32[2,16,8,256]{3,2,1,0:T(8,128)}, f3...) custom-call(s32[3]{0:T(128)} %pad_add_fusion.scalars, f32[7,40,40,256]{3,2,1,0:T(8,128)} %get-tuple-element.31.coef, ...), custom_call_target="tpu_custom_call" | custom-call | flops 36700160 | bytes 18415628 | tf_op jit(solution)/shard_map/pallas_call | solution.py:21
  279.5 3.1 collective-permute-start.15
  282.6 1.3 collective-permute-start.16
  283.9 1.9 collective-permute-start.17
  285.8 0.6 pad_add_fusion.3.scalars
  286.4 2.6 collective-permute-start.18
  289.7 3.5 collective-permute-done.18.refs_3_
  293.2 1.3 collective-permute-start.19
  295.1 3.6 collective-permute-done.19.refs_4_
  299.6 33.1 %shard_map.63.second = f32[2,32,32,256]{3,2,1,0:T(8,128)} custom-call(s32[3]{0:T(128)} %pad_add_fusion.scalars, f32[7,40,40,256]{3,2,1,0:T(8,128)} %get-tuple-element.31.coef, f32[2,32,32,256]{3,2,1,0:T(8,128)} %get-tuple-element.44.tile, f32[32,32,256]{2,1,0:T(8,128)} %weight.7, f32[2,4,32,256]{3,2,1,0:T(8,128)} %copy-done.4, f32[2,4,32,256]{3,2,1,0:T(8,128)} %copy-done.7, ...), custom_call_target="tpu_custom_call" | custom-call | flops 36700160 | bytes 17563660 | tf_op jit(solution)/shard_map/pallas_call | solution.py:21
  332.6 4.1 %shard_map.64 = f32[8,128]{1,0:T(8,128)} custom-call(s32[3]{0:T(128)} %pad_add_fusion.scalars, f32[2,32,32,256]{3,2,1,0:T(8,128)} %get-tuple-element.38.tile.images.others.refs_0_, f32[2,32,32,256]{3,2,1,0:T(8,128)} %shard_map.63.second, f32[2,32,32,256]{3,2,1,0:T(8,128)} %get-tuple-element.38.tile.images.others.refs_0_), custom_call_target="tpu_custom_call" | custom-call | flops 2097152 | bytes 6295564 | tf_op jit(solution)/shard_map/pallas_call | solution.py:21
  336.8 4.3 %shard_map.65 = f32[8,128]{1,0:T(8,128)} custom-call(s32[3]{0:T(128)} %pad_add_fusion.2.scalars, f32[2,32,32,256]{3,2,1,0:T(8,128)} %get-tuple-element.38.tile.images.others.refs_0_, f32[2,32,32,256]{3,2,1,0:T(8,128)} %shard_map.63.second, f32[2,32,32,256]{3,2,1,0:T(8,128)} %copy-done), custom_call_target="tpu_custom_call" | custom-call | flops 2097152 | bytes 6295564 | tf_op jit(solution)/shard_map/pallas_call | solution.py:21
  341.0 0.7 add.79
  341.8 4.2 %shard_map.66 = f32[8,128]{1,0:T(8,128)} custom-call(s32[3]{0:T(128)} %pad_add_fusion.3.scalars, f32[2,32,32,256]{3,2,1,0:T(8,128)} %get-tuple-element.38.tile.images.others.refs_0_, f32[2,32,32,256]{3,2,1,0:T(8,128)} %shard_map.63.second, f32[2,32,32,256]{3,2,1,0:T(8,128)} %collective-permute-done.21.others.refs_2_), custom_call_target="tpu_custom_call" | custom-call | flops 2097152 | bytes 6295564 | tf_op jit(solution)/shard_map/pallas_call | solution.py:21
  346.1 0.8 copy.17
  346.8 4.2 %shard_map.67 = f32[8,128]{1,0:T(8,128)} custom-call(s32[3]{0:T(128)} %pad_add_fusion.4.scalars, f32[2,32,32,256]{3,2,1,0:T(8,128)} %get-tuple-element.38.tile.images.others.refs_0_, f32[2,32,32,256]{3,2,1,0:T(8,128)} %shard_map.63.second, f32[2,32,32,256]{3,2,1,0:T(8,128)} %collective-permute-done.22.others.refs_3_), custom_call_target="tpu_custom_call" | custom-call | flops 2097152 | bytes 6295564 | tf_op jit(solution)/shard_map/pallas_call | solution.py:21
  351.1 0.8 copy.18
  351.9 1.3 collective-permute-start.23
  353.2 0.9 collective-permute-done.23
  354.1 1.0 collective-permute-start.24
  355.1 3.4 collective-permute-done.24
  358.5 1.9 collective-permute-start.25
  360.4 2.4 collective-permute-done.25
  362.8 0.7 collective-permute-start.26
  363.6 3.6 collective-permute-done.26
  367.2 1.9 collective-permute-start.27
  369.1 4.0 %collective-permute-done.27 = f32[8,128]{0,1:T(8,128)S(1)} collective-permute-done((f32[8,128]{0,1:T(8,128)S(1)}, f32[8,128]{0,1:T(8,128)S(1)}, u32[]{:S(2)}, u32[]{:S(2)}) %collective-permute-start.27) | collective-permute-done | bytes 4128 | tf_op jit(solution)/shard_map/ppermute | solution.py:341
  373.5 0.7 cholesky.16
  374.3 0.6 compare_reduce_fusion
  374.9 0.6 fusion
  376.6 0.7 fusion.17
  377.5 0.7 pad_maximum_fusion.inverse
  378.1 6.1 %shard_map.68 = f32[2,32,32,256]{3,2,1,0:T(8,128)} custom-call(f32[2,8]{1,0:T(2,128)} %pad_maximum_fusion.inverse, f32[2,32,32,256]{3,2,1,0:T(8,128)} %get-tuple-element.38.tile.images.others.refs_0_, f32[2,32,32,256]{3,2,1,0:T(8,128)} %copy-done, f32[2,32,32,256]{3,2,1,0:T(8,128)} %collective-permute-done.21.others.refs_2_, ...), custom_call_target="tpu_custom_call" | custom-call | flops 8388608 | bytes 10485824 | tf_op jit(solution)/shard_map/pallas_call | solution.py:21
  (79 shorter events, 7.4 us)
Async XLA Ops:
  6.2 27.9 %collective-permute-start = (f32[6,4,32,256]{3,2,1,0:T(8,128)}, f32[6,4,32,256]{3,2,1,0:T(8,128)S(1)}, u32[]{:S(2)}, u32[]{:S(2)}) collective-permute-start(f32[6,4,32,256]{3,2,1,0:T(8,128)} %get-tuple-element.26), channel_id=1, source_target_pairs={{0,2},{2,4},{4,6},{1,3},{3,5},{5,7},{8,10},{10,12},{12,14},{9,11},... | collective-permute-start | bytes 2359304 | tf_op jit(solution)/shard_map/ppermute | solution.py:82
  8.6 25.5 %collective-permute-start.1 = (f32[6,4,32,256]{3,2,1,0:T(8,128)}, f32[6,4,32,256]{3,2,1,0:T(8,128)S(1)}, u32[]{:S(2)}, u32[]{:S(2)}) collective-permute-start(f32[6,4,32,256]{3,2,1,0:T(8,128)} %get-tuple-element.27), channel_id=1, source_target_pairs={{2,0},{4,2},{6,4},{3,1},{5,3},{7,5},{10,8},{12,10},{14,12},{11,9},... | collective-permute-start | bytes 2359304 | tf_op jit(solution)/shard_map/ppermute | solution.py:83
  9.9 24.2 %collective-permute-start.2 = (f32[6,16,8,256]{3,2,1,0:T(8,128)}, f32[6,16,8,256]{3,2,1,0:T(8,128)S(1)}, u32[]{:S(2)}, u32[]{:S(2)}) collective-permute-start(f32[6,16,8,256]{3,2,1,0:T(8,128)} %get-tuple-element.28), channel_id=1, source_target_pairs={{0,1},{1,0},{2,3},{3,2},{4,5},{5,4},{6,7},{7,6},{8,9},{9,8},{10,11... | collective-permute-start | bytes 2359304 | tf_op jit(solution)/shard_map/ppermute | solution.py:80
  12.4 20.0 %collective-permute-start.3 = (f32[6,2,8,256]{3,2,1,0:T(8,128)}, f32[6,2,8,256]{3,2,1,0:T(8,128)S(1)}, u32[]{:S(2)}, u32[]{:S(2)}) collective-permute-start(f32[6,2,8,256]{3,2,1,0:T(8,128)} %get-tuple-element.29), channel_id=1, source_target_pairs={{0,3},{1,2},{2,5},{3,4},{4,7},{5,6},{8,11},{9,10},{10,13},{11,12},... | collective-permute-start | bytes 294920 | tf_op jit(solution)/shard_map/ppermute | solution.py:80
  16.5 17.7 %collective-permute-start.4 = (f32[6,2,8,256]{3,2,1,0:T(8,128)}, f32[6,2,8,256]{3,2,1,0:T(8,128)S(1)}, u32[]{:S(2)}, u32[]{:S(2)}) collective-permute-start(f32[6,2,8,256]{3,2,1,0:T(8,128)} %get-tuple-element.30), channel_id=1, source_target_pairs={{2,1},{3,0},{4,3},{5,2},{6,5},{7,4},{10,9},{11,8},{12,11},{13,10},... | collective-permute-start | bytes 294920 | tf_op jit(solution)/shard_map/ppermute | solution.py:80
  32.3 1.8 copy-start.13
  34.1 0.6 copy-start.14
  34.1 1.0 copy-start.1
  34.1 1.3 copy-start.2
  35.4 0.9 copy-start.3
  74.0 14.4 %collective-permute-start.5 = (f32[2,4,32,256]{3,2,1,0:T(8,128)}, f32[2,4,32,256]{3,2,1,0:T(8,128)S(1)}, u32[]{:S(2)}, u32[]{:S(2)}) collective-permute-start(f32[2,4,32,256]{3,2,1,0:T(8,128)} %get-tuple-element.33), channel_id=1, source_target_pairs={{0,2},{2,4},{4,6},{1,3},{3,5},{5,7},{8,10},{10,12},{12,14},{9,11},... | collective-permute-start | bytes 786440 | tf_op jit(solution)/shard_map/ppermute | solution.py:82
  75.6 12.8 %collective-permute-start.6 = (f32[2,4,32,256]{3,2,1,0:T(8,128)}, f32[2,4,32,256]{3,2,1,0:T(8,128)S(1)}, u32[]{:S(2)}, u32[]{:S(2)}) collective-permute-start(f32[2,4,32,256]{3,2,1,0:T(8,128)} %get-tuple-element.34), channel_id=1, source_target_pairs={{2,0},{4,2},{6,4},{3,1},{5,3},{7,5},{10,8},{12,10},{14,12},{11,9},... | collective-permute-start | bytes 786440 | tf_op jit(solution)/shard_map/ppermute | solution.py:83
  76.9 11.5 %collective-permute-start.7 = (f32[2,16,8,256]{3,2,1,0:T(8,128)}, f32[2,16,8,256]{3,2,1,0:T(8,128)S(1)}, u32[]{:S(2)}, u32[]{:S(2)}) collective-permute-start(f32[2,16,8,256]{3,2,1,0:T(8,128)} %get-tuple-element.35), channel_id=1, source_target_pairs={{0,1},{1,0},{2,3},{3,2},{4,5},{5,4},{6,7},{7,6},{8,9},{9,8},{10,11... | collective-permute-start | bytes 786440 | tf_op jit(solution)/shard_map/ppermute | solution.py:80
  78.6 7.4 %collective-permute-start.8 = (f32[2,2,8,256]{3,2,1,0:T(8,128)}, f32[2,2,8,256]{3,2,1,0:T(8,128)S(1)}, u32[]{:S(2)}, u32[]{:S(2)}) collective-permute-start(f32[2,2,8,256]{3,2,1,0:T(8,128)} %get-tuple-element.36), channel_id=1, source_target_pairs={{0,3},{1,2},{2,5},{3,4},{4,7},{5,6},{8,11},{9,10},{10,13},{11,12},... | collective-permute-start | bytes 98312 | tf_op jit(solution)/shard_map/ppermute | solution.py:80
  82.7 5.7 %collective-permute-start.9 = (f32[2,2,8,256]{3,2,1,0:T(8,128)}, f32[2,2,8,256]{3,2,1,0:T(8,128)S(1)}, u32[]{:S(2)}, u32[]{:S(2)}) collective-permute-start(f32[2,2,8,256]{3,2,1,0:T(8,128)} %get-tuple-element.37), channel_id=1, source_target_pairs={{2,1},{3,0},{4,3},{5,2},{6,5},{7,4},{10,9},{11,8},{12,11},{13,10},... | collective-permute-start | bytes 98312 | tf_op jit(solution)/shard_map/ppermute | solution.py:80
  86.0 2.4 copy-start.16
  88.4 0.6 copy-start.18
  88.4 0.7 copy-start.6
  88.4 0.8 copy-start.9
  88.4 0.9 copy-start.12
  122.9 48.2 %collective-permute-start.20 = (f32[2,32,32,256]{3,2,1,0:T(8,128)}, f32[2,32,32,256]{3,2,1,0:T(8,128)S(1)}, u32[]{:S(2)}, u32[]{:S(2)}) collective-permute-start(f32[2,32,32,256]{3,2,1,0:T(8,128)} %get-tuple-element.38.tile.images.others.refs_0_), channel_id=1, source_target_pairs={{0,8},{8,16},{16,24},{1,9},{9,17},{17,25},{2,10},{10,18},{18,26},{... | collective-permute-start | bytes 6291464 | tf_op jit(solution)/shard_map/ppermute | solution.py:389
  171.1 108.4 %copy-start = (f32[2,32,32,256]{3,2,1,0:T(8,128)}, f32[2,32,32,256]{3,2,1,0:T(8,128)S(1)}, u32[]{:S(2)}) copy-start(f32[2,32,32,256]{3,2,1,0:T(8,128)S(1)} %collective-permute-done.20.others.refs_1_) | copy-start | bytes 6291460
  171.1 49.9 %collective-permute-start.21 = (f32[2,32,32,256]{3,2,1,0:T(8,128)S(1)}, f32[2,32,32,256]{3,2,1,0:T(8,128)}, u32[]{:S(2)}, u32[]{:S(2)}) collective-permute-start(f32[2,32,32,256]{3,2,1,0:T(8,128)S(1)} %collective-permute-done.20.others.refs_1_), channel_id=1, source_target_pairs={{0,8},{8,16},{16,24},{1,9},{9,17},{17,25},{2,10},{10,18},{18,26},{... | collective-permute-start | bytes 6291464 | tf_op jit(solution)/shard_map/ppermute | solution.py:389
  221.0 125.9 %collective-permute-start.22 = (f32[2,32,32,256]{3,2,1,0:T(8,128)}, f32[2,32,32,256]{3,2,1,0:T(8,128)}, u32[]{:S(2)}, u32[]{:S(2)}) collective-permute-start(f32[2,32,32,256]{3,2,1,0:T(8,128)} %collective-permute-done.21.others.refs_2_), channel_id=1, source_target_pairs={{0,8},{8,16},{16,24},{1,9},{9,17},{17,25},{2,10},{10,18},{18,26},{... | collective-permute-start | bytes 6291464 | tf_op jit(solution)/shard_map/ppermute | solution.py:389
  226.8 17.9 %collective-permute-start.10 = (f32[2,4,32,256]{3,2,1,0:T(8,128)}, f32[2,4,32,256]{3,2,1,0:T(8,128)S(1)}, u32[]{:S(2)}, u32[]{:S(2)}) collective-permute-start(f32[2,4,32,256]{3,2,1,0:T(8,128)} %get-tuple-element.39), channel_id=1, source_target_pairs={{0,2},{2,4},{4,6},{1,3},{3,5},{5,7},{8,10},{10,12},{12,14},{9,11},... | collective-permute-start | bytes 786440 | tf_op jit(solution)/shard_map/ppermute | solution.py:82
  228.6 16.1 %collective-permute-start.11 = (f32[2,4,32,256]{3,2,1,0:T(8,128)}, f32[2,4,32,256]{3,2,1,0:T(8,128)S(1)}, u32[]{:S(2)}, u32[]{:S(2)}) collective-permute-start(f32[2,4,32,256]{3,2,1,0:T(8,128)} %get-tuple-element.40), channel_id=1, source_target_pairs={{2,0},{4,2},{6,4},{3,1},{5,3},{7,5},{10,8},{12,10},{14,12},{11,9},... | collective-permute-start | bytes 786440 | tf_op jit(solution)/shard_map/ppermute | solution.py:83
  229.9 14.8 %collective-permute-start.12 = (f32[2,16,8,256]{3,2,1,0:T(8,128)}, f32[2,16,8,256]{3,2,1,0:T(8,128)S(1)}, u32[]{:S(2)}, u32[]{:S(2)}) collective-permute-start(f32[2,16,8,256]{3,2,1,0:T(8,128)} %get-tuple-element.41), channel_id=1, source_target_pairs={{0,1},{1,0},{2,3},{3,2},{4,5},{5,4},{6,7},{7,6},{8,9},{9,8},{10,11... | collective-permute-start | bytes 786440 | tf_op jit(solution)/shard_map/ppermute | solution.py:80
  231.8 7.4 %collective-permute-start.13 = (f32[2,2,8,256]{3,2,1,0:T(8,128)}, f32[2,2,8,256]{3,2,1,0:T(8,128)S(1)}, u32[]{:S(2)}, u32[]{:S(2)}) collective-permute-start(f32[2,2,8,256]{3,2,1,0:T(8,128)} %get-tuple-element.42), channel_id=1, source_target_pairs={{0,3},{1,2},{2,5},{3,4},{4,7},{5,6},{8,11},{9,10},{10,13},{11,12},... | collective-permute-start | bytes 98312 | tf_op jit(solution)/shard_map/ppermute | solution.py:80
  239.2 5.5 %copy-start.15 = (f32[2,2,8,256]{3,2,1,0:T(8,128)}, f32[2,2,8,256]{3,2,1,0:T(8,128)S(1)}, u32[]{:S(2)}) copy-start(f32[2,2,8,256]{3,2,1,0:T(8,128)S(1)} %collective-permute-done.13.refs_3_) | copy-start | bytes 98308
  239.2 5.5 %collective-permute-start.14 = (f32[2,2,8,256]{3,2,1,0:T(8,128)}, f32[2,2,8,256]{3,2,1,0:T(8,128)S(1)}, u32[]{:S(2)}, u32[]{:S(2)}) collective-permute-start(f32[2,2,8,256]{3,2,1,0:T(8,128)} %get-tuple-element.43), channel_id=1, source_target_pairs={{2,1},{3,0},{4,3},{5,2},{6,5},{7,4},{10,9},{11,8},{12,11},{13,10},... | collective-permute-start | bytes 98312 | tf_op jit(solution)/shard_map/ppermute | solution.py:80
  244.7 0.6 copy-start.19
  244.7 0.7 copy-start.5
  244.7 0.8 copy-start.8
  245.5 0.7 copy-start.11
  279.5 19.2 %collective-permute-start.15 = (f32[2,4,32,256]{3,2,1,0:T(8,128)}, f32[2,4,32,256]{3,2,1,0:T(8,128)S(1)}, u32[]{:S(2)}, u32[]{:S(2)}) collective-permute-start(f32[2,4,32,256]{3,2,1,0:T(8,128)} %get-tuple-element.45), channel_id=1, source_target_pairs={{0,2},{2,4},{4,6},{1,3},{3,5},{5,7},{8,10},{10,12},{12,14},{9,11},... | collective-permute-start | bytes 786440 | tf_op jit(solution)/shard_map/ppermute | solution.py:82
  282.6 16.1 %collective-permute-start.16 = (f32[2,4,32,256]{3,2,1,0:T(8,128)}, f32[2,4,32,256]{3,2,1,0:T(8,128)S(1)}, u32[]{:S(2)}, u32[]{:S(2)}) collective-permute-start(f32[2,4,32,256]{3,2,1,0:T(8,128)} %get-tuple-element.46), channel_id=1, source_target_pairs={{2,0},{4,2},{6,4},{3,1},{5,3},{7,5},{10,8},{12,10},{14,12},{11,9},... | collective-permute-start | bytes 786440 | tf_op jit(solution)/shard_map/ppermute | solution.py:83
  283.9 14.8 %collective-permute-start.17 = (f32[2,16,8,256]{3,2,1,0:T(8,128)}, f32[2,16,8,256]{3,2,1,0:T(8,128)S(1)}, u32[]{:S(2)}, u32[]{:S(2)}) collective-permute-start(f32[2,16,8,256]{3,2,1,0:T(8,128)} %get-tuple-element.47), channel_id=1, source_target_pairs={{0,1},{1,0},{2,3},{3,2},{4,5},{5,4},{6,7},{7,6},{8,9},{9,8},{10,11... | collective-permute-start | bytes 786440 | tf_op jit(solution)/shard_map/ppermute | solution.py:80
  286.4 6.7 %collective-permute-start.18 = (f32[2,2,8,256]{3,2,1,0:T(8,128)}, f32[2,2,8,256]{3,2,1,0:T(8,128)S(1)}, u32[]{:S(2)}, u32[]{:S(2)}) collective-permute-start(f32[2,2,8,256]{3,2,1,0:T(8,128)} %get-tuple-element.48), channel_id=1, source_target_pairs={{0,3},{1,2},{2,5},{3,4},{4,7},{5,6},{8,11},{9,10},{10,13},{11,12},... | collective-permute-start | bytes 98312 | tf_op jit(solution)/shard_map/ppermute | solution.py:80
  293.2 5.5 %copy-start.17 = (f32[2,2,8,256]{3,2,1,0:T(8,128)}, f32[2,2,8,256]{3,2,1,0:T(8,128)S(1)}, u32[]{:S(2)}) copy-start(f32[2,2,8,256]{3,2,1,0:T(8,128)S(1)} %collective-permute-done.18.refs_3_) | copy-start | bytes 98308
  293.2 5.5 %collective-permute-start.19 = (f32[2,2,8,256]{3,2,1,0:T(8,128)}, f32[2,2,8,256]{3,2,1,0:T(8,128)S(1)}, u32[]{:S(2)}, u32[]{:S(2)}) collective-permute-start(f32[2,2,8,256]{3,2,1,0:T(8,128)} %get-tuple-element.49), channel_id=1, source_target_pairs={{2,1},{3,0},{4,3},{5,2},{6,5},{7,4},{10,9},{11,8},{12,11},{13,10},... | collective-permute-start | bytes 98312 | tf_op jit(solution)/shard_map/ppermute | solution.py:80
  298.7 0.6 copy-start.20
  298.7 0.7 copy-start.4
  298.7 0.8 copy-start.7
  298.7 0.9 copy-start.10
  336.8 4.3 %copy-start.21 = (f32[8,128]{1,0:T(8,128)S(1)}, f32[8,128]{1,0:T(8,128)}, u32[]{:S(2)}) copy-start(f32[8,128]{1,0:T(8,128)} %shard_map.64) | copy-start | bytes 12292
  351.9 2.2 collective-permute-start.23
  354.1 4.4 %collective-permute-start.24 = (f32[8,128]{0,1:T(8,128)S(1)}, f32[8,128]{0,1:T(8,128)S(1)}, u32[]{:S(2)}, u32[]{:S(2)}) collective-permute-start(f32[8,128]{0,1:T(8,128)S(1)} %add.82), channel_id=1, source_target_pairs={{0,4},{2,6},{4,0},{6,2},{1,5},{3,7},{5,1},{7,3},{8,12},{10,14},{12... | collective-permute-start | bytes 12296 | tf_op jit(solution)/shard_map/ppermute | solution.py:341
  358.5 4.3 %collective-permute-start.25 = (f32[8,128]{0,1:T(8,128)S(1)}, f32[8,128]{0,1:T(8,128)S(1)}, u32[]{:S(2)}, u32[]{:S(2)}) collective-permute-start(f32[8,128]{0,1:T(8,128)S(1)} %add.83), channel_id=1, source_target_pairs={{0,1},{1,0},{2,3},{3,2},{4,5},{5,4},{6,7},{7,6},{8,9},{9,8},{10,11... | collective-permute-start | bytes 12296 | tf_op jit(solution)/shard_map/ppermute | solution.py:341
  362.8 4.3 %collective-permute-start.26 = (f32[8,128]{0,1:T(8,128)S(1)}, f32[8,128]{0,1:T(8,128)S(1)}, u32[]{:S(2)}, u32[]{:S(2)}) collective-permute-start(f32[8,128]{0,1:T(8,128)S(1)} %add.84), channel_id=1, source_target_pairs={{0,8},{8,0},{16,24},{24,16},{1,9},{9,1},{17,25},{25,17},{2,10},{10... | collective-permute-start | bytes 12296 | tf_op jit(solution)/shard_map/ppermute | solution.py:341
  367.2 5.9 %collective-permute-start.27 = (f32[8,128]{0,1:T(8,128)S(1)}, f32[8,128]{0,1:T(8,128)S(1)}, u32[]{:S(2)}, u32[]{:S(2)}) collective-permute-start(f32[8,128]{0,1:T(8,128)S(1)} %add.85), channel_id=1, source_target_pairs={{0,16},{8,24},{16,0},{24,8},{1,17},{9,25},{17,1},{25,9},{2,18},{10... | collective-permute-start | bytes 12296 | tf_op jit(solution)/shard_map/ppermute | solution.py:341
